TPU v7x, 128 devices: a whole 4x4x4 slice. The times are simulated.
128 devices in a mesh: tm: 8 (over z, core), space: 16 (over x, y).
Axes of the slice: x: 4, y: 4, z: 4, core: 2. Of those that a mesh axis runs over, the one named last changes fastest.
Arguments:
- features: bfloat16 [8, 64, 1536, 512], P('tm', None, 'space'), may hold values from -6 to 6
- pre_act: bfloat16 [8, 64, 1536, 512], P('tm', None, 'space'), may hold values from -6 to 6
- cotangent: bfloat16 [8, 64, 1536, 512], P('tm', None, 'space'), may hold values from -6 to 6
- first_weight: bfloat16 [9, 64, 64], replicated, may hold values from -0.25 to 0.25
- second_weight: bfloat16 [9, 64, 64], replicated, may hold values from -0.25 to 0.25
- tile_mask: int32 [8, 48, 16], P('tm'), may hold values from 0 to 1, as said below
- tile_list: int32 [8, 512], P('tm', 'space'), may hold values from 0 to 47, as said below
Outputs:
- input_grad: bfloat16 [8, 64, 1536, 512], P('tm', None, 'space')
- first_grad: float32 [9, 64, 64], replicated
- second_grad: float32 [9, 64, 64], replicated
Inputs may be any that keep to these rules, and one draw needn't show every extreme that they name: `tile_mask`: within each hour, every block of 3 tile rows holds at least 8 and at most 32 active tiles, and some block holds exactly 32; two blocks whose indices differ by half the number of blocks hold at most 40 active tiles together, and some such pair holds exactly that. In each hour one column has active tiles in the first and the last tile row of every block. `tile_list`: for each hour and block b, entries b * 32 to b * 32 + 31 are distinct local tile numbers of block b: first all its active tiles in increasing order, then inactive ones in increasing order.
All inputs are finite; a program needn't handle non-finite values.
Results may differ from a plain program's by a relative error of at most 0.0085.
Values may be sent and summed in bfloat16 or wider, within the bound.
A program may use at most 256 MiB of HBM per device.

v0:
```python
import math

import jax
import jax.numpy as jnp
from jax import lax
from jax.sharding import PartitionSpec as P

TS = 32
WINDOW_COLS = 1280


def with_halo(shard, sides, width):
    for axis, dim in sides:
        devices, length = (lax.axis_size(axis), shard.shape[dim])
        up = [(i, (i + 1) % devices) for i in range(devices - 1)]
        down = [(j, i) for i, j in up]
        last = lax.slice_in_dim(shard, length - width, length, axis=dim)
        leading = lax.slice_in_dim(shard, 0, width, axis=dim)
        before = lax.ppermute(last, axis, up)
        after = lax.ppermute(leading, axis, down)
        shard = jnp.concatenate([before, shard, after], axis=dim)
    return shard


def shortened(shard):
    return jax.tree.map(lambda a: a.astype(jnp.bfloat16) if a.dtype == jnp.float32 else a, shard)


def tile_layout(dense_field, tile_side):
    hour_total, channels, cell_rows, cell_cols = dense_field.shape
    grid_rows = cell_rows // tile_side
    grid_cols = cell_cols // tile_side
    shaped = dense_field.reshape(hour_total, channels, grid_rows, tile_side, grid_cols, tile_side)
    shaped = shaped.transpose(0, 2, 4, 1, 3, 5)
    return shaped.reshape(hour_total, grid_rows * grid_cols, channels, tile_side * tile_side)


def dense_layout(tile_field, cell_rows, cell_cols, tile_side):
    hour_total = tile_field.shape[0]
    channels = tile_field.shape[2]
    grid_rows = cell_rows // tile_side
    grid_cols = cell_cols // tile_side
    shaped = tile_field.reshape(hour_total, grid_rows, grid_cols, channels, tile_side, tile_side)
    shaped = shaped.transpose(0, 3, 1, 4, 2, 5)
    return shaped.reshape(hour_total, channels, cell_rows, cell_cols)


def place_slots(slot_values, slot_ids, tile_total):

    def fill_hour(hour_values, hour_ids):
        canvas = jnp.zeros((tile_total,) + hour_values.shape[1:], hour_values.dtype)
        return canvas.at[hour_ids].set(hour_values, mode="promise_in_bounds")

    return jax.vmap(fill_hour)(slot_values, slot_ids)


def pick_slots(tile_field, slot_ids):
    return jnp.take_along_axis(tile_field, slot_ids[:, :, None, None], axis=1, mode="clip")


def frame_windows(dense_field, slot_ids, tile_side, grid_cols, padded_cols):
    channels = dense_field.shape[1]
    extent = tile_side + 2
    framed = jnp.pad(dense_field, ((0, 0), (0, 0), (0, 0), (1, 1)))

    def single(hour_plane, tile_id):
        anchor = jnp.zeros((), jnp.int32)
        window = lax.dynamic_slice(
            hour_plane,
            (anchor, tile_id // grid_cols * tile_side, tile_id % grid_cols * tile_side),
            (channels, extent, extent),
        )
        flat_window = window.reshape(channels, extent * extent)
        return jnp.pad(flat_window, ((0, 0), (0, padded_cols - extent * extent)))

    def per_hour(hour_plane, hour_ids):
        return jax.vmap(lambda tile_id: single(hour_plane, tile_id))(hour_ids)

    return jax.vmap(per_hour)(framed, slot_ids)


def shifted_stack(windows, tile_side):
    slot_total, channels = (windows.shape[0], windows.shape[1])
    extent = tile_side + 2
    grid_view = windows[:, :, : extent * extent].reshape(slot_total, channels, extent, extent)
    pieces = []
    for step_row in (-1, 0, 1):
        for step_col in (-1, 0, 1):
            shifted = grid_view[
                :,
                :,
                1 - step_row : 1 - step_row + tile_side,
                1 - step_col : 1 - step_col + tile_side,
            ]
            pieces.append(shifted.reshape(slot_total, channels, tile_side * tile_side))
    return jnp.concatenate(pieces, axis=1)


def second_layer(weight_rows, tile_side, operands):
    windows, kept_tiles = (operands[0], operands[1])
    stacked = shifted_stack(windows, tile_side)
    upstream = jnp.einsum("ik,skq->siq", weight_rows, stacked, preferred_element_type=jnp.float32)
    positive = (kept_tiles > 0).astype(jnp.float32)
    pre_tiles = (upstream * positive).astype(jnp.bfloat16)
    partial_grad = jnp.einsum(
        "skq,siq->ki", stacked, kept_tiles, preferred_element_type=jnp.float32
    )
    return (pre_tiles, partial_grad)


def first_layer(weight_rows, tile_side, operands):
    windows, input_tiles, slot_mask = operands
    stacked = shifted_stack(windows, tile_side)
    downstream = jnp.einsum("ik,skq->siq", weight_rows, stacked, preferred_element_type=jnp.float32)
    result_tiles = (downstream * slot_mask[:, None, None]).astype(jnp.bfloat16)
    partial_grad = jnp.einsum(
        "skq,siq->ki", stacked, input_tiles, preferred_element_type=jnp.float32
    )
    return (result_tiles, partial_grad)


def spread_layer(layer_fn, windows, tiles, slot_mask):
    aligned, partial_grads = lax.map(layer_fn, (windows, tiles, slot_mask))
    return (aligned, jnp.sum(partial_grads, axis=0))


def shards(features, pre_act, cotangent, first_weight, second_weight, tile_mask, tile_list):
    hour_total, channels, cell_rows, cell_cols = features.shape
    tile_side = TS
    grid_cols = cell_cols // tile_side
    block_rows = cell_rows // tile_side
    tile_total = block_rows * grid_cols
    space_size = lax.axis_size("space")
    my_index = lax.axis_index("space")
    own_mask = lax.dynamic_slice_in_dim(tile_mask, my_index * block_rows, block_rows, 1)
    cell_mask = jnp.repeat(jnp.repeat(own_mask, tile_side, axis=1), tile_side, axis=2)[
        :, None
    ].astype(jnp.bfloat16)
    grad_out = cotangent * cell_mask
    kept_field = jnp.maximum(pre_act, jnp.zeros((), jnp.bfloat16)) * cell_mask
    input_kept = features * cell_mask
    slot_mask = jnp.take_along_axis(
        own_mask.reshape(hour_total, tile_total), tile_list, axis=1, mode="clip"
    ).astype(jnp.float32)
    second_rows = second_weight.transpose(2, 0, 1).reshape(channels, 9 * channels)
    first_rows = first_weight.transpose(2, 0, 1).reshape(channels, 9 * channels)
    grad_frame = with_halo(grad_out, (("space", 2),), 1)
    grad_windows = frame_windows(grad_frame, tile_list, tile_side, grid_cols, WINDOW_COLS)
    kept_tiles = pick_slots(tile_layout(kept_field, tile_side), tile_list)
    pre_slots, second_part = spread_layer(
        lambda operands: second_layer(second_rows, tile_side, operands),
        grad_windows,
        kept_tiles,
        slot_mask,
    )
    pre_grad = dense_layout(
        place_slots(pre_slots, tile_list, tile_total), cell_rows, cell_cols, tile_side
    )
    pre_frame = with_halo(shortened(pre_grad), (("space", 2),), 1).astype(pre_grad.dtype)
    pre_windows = frame_windows(pre_frame, tile_list, tile_side, grid_cols, WINDOW_COLS)
    input_tiles = pick_slots(tile_layout(input_kept, tile_side), tile_list)
    input_slots, first_part = spread_layer(
        lambda operands: first_layer(first_rows, tile_side, operands),
        pre_windows,
        input_tiles,
        slot_mask,
    )
    first_grad, second_grad = lax.psum((first_part, second_part), ("tm", "space"))
    input_grad = dense_layout(
        place_slots(input_slots, tile_list, tile_total), cell_rows, cell_cols, tile_side
    )
    cell_total = hour_total * lax.axis_size("tm") * cell_rows * space_size * cell_cols
    grad_scale = 1.0 / math.sqrt(cell_total)
    first_grad = (first_grad * grad_scale).reshape(9, channels, channels)
    second_grad = (second_grad * grad_scale).reshape(9, channels, channels)
    return (input_grad, first_grad, second_grad)


def solution(mesh):
    return jax.shard_map(
        shards,
        mesh=mesh,
        in_specs=(
            P("tm", None, "space", None),
            P("tm", None, "space", None),
            P("tm", None, "space", None),
            P(),
            P(),
            P("tm", None, None),
            P("tm", "space"),
        ),
        out_specs=(P("tm", None, "space", None), P(), P()),
        check_vma=False,
    )
```

profile of v0, /device:TPU:1, one launch (start us, length us, event | category | flops | bytes accessed | tf_op | source)
XLA Modules:
  0.0 1932.6 jit_solution(10434787184210081423)
XLA Ops:
  48.2 26.7 %broadcast_multiply_fusion = (bf16[1,64,96,512]{1,3,2,0:T(8,128)(2,1)}, bf16[1,64,96,512]{1,3,2,0:T(8,128)(2,1)}, bf16[1,64,96,512]{1,3,2,0:T(8,128)(2,1)}) fusion(bf16[1,64,96,512]{1,3,2,0:T(8,128)(2,1)} %copy.190, bf16[96,512]{1,0:T(8,128)(2,1)S(1)} %copy.140, bf16[1,64,96,512]{1,3,2,0:T(8,128)(2,1)} %copy.143, bf16[1,64,96,512]{1,3,2,0:T(8,128)(2,1)} %copy.137), kind=kLoop, calls=%fused_computation.25 | loop fusion | flops 12582912 | bytes 37847040 | tf_op jit(solution)/shard_map/mul | solution.py:141
  133.4 15.4 fusion.5
  154.6 601.5 %while.2 = (s32[]{:T(128)}, bf16[1,64,98,514]{1,3,2,0:T(8,128)(2,1)}, s32[32,4]{0,1:T(4,128)S(1)}, bf16[32,64,34,34]{1,0,3,2:T(8,128)(2,1)}, s32[]{:T(128)}, /*index=5*/s32[]{:T(128)}) while((s32[]{:T(128)}, bf16[1,64,98,514]{1,3,2,0:T(8,128)(2,1)}, s32[32,4]{0,1:T(4,128)S(1)}, bf16[32,64,34,34]{1,0,3,2:T(8,128)(2,1)}, s32[]{:T(128)}, ...), condition=%wide.while_cond, body=%wide.while_body.sunk | while | flops 2 | bytes 887949 | solution.py:68
  158.1 15.3 dynamic-update-slice.42
  176.9 15.3 dynamic-update-slice.42
  195.7 15.3 dynamic-update-slice.42
  214.5 15.3 dynamic-update-slice.42
  233.3 15.3 dynamic-update-slice.42
  252.1 15.3 dynamic-update-slice.42
  270.9 15.3 dynamic-update-slice.42
  289.7 15.3 dynamic-update-slice.42
  308.5 15.3 dynamic-update-slice.42
  327.3 15.3 dynamic-update-slice.42
  346.1 15.3 dynamic-update-slice.42
  364.9 15.3 dynamic-update-slice.42
  383.7 15.3 dynamic-update-slice.42
  402.5 15.3 dynamic-update-slice.42
  421.3 15.3 dynamic-update-slice.42
  440.1 15.3 dynamic-update-slice.42
  458.9 15.3 dynamic-update-slice.42
  477.7 15.3 dynamic-update-slice.42
  496.5 15.3 dynamic-update-slice.42
  515.3 15.3 dynamic-update-slice.42
  534.0 15.3 dynamic-update-slice.42
  552.8 15.3 dynamic-update-slice.42
  571.6 15.3 dynamic-update-slice.42
  590.4 15.3 dynamic-update-slice.42
  628.0 15.3 dynamic-update-slice.42
  665.6 15.3 dynamic-update-slice.42
  703.2 15.3 dynamic-update-slice.42
  740.8 15.3 dynamic-update-slice.42
  764.3 23.8 %fusion.20 = (bf16[32,64,32,32]{1,0,3,2:T(8,128)(2,1)}, bf16[32,64,32,32]{1,0,3,2:T(8,128)(2,1)}, bf16[32,64,32,32]{1,0,3,2:T(8,128)(2,1)}, bf16[32,64,32,32]{1,...) fusion(bf16[32,64,34,34]{1,0,3,2:T(8,128)(2,1)S(1)} %bitcast.111), kind=kLoop, calls=%fused_computation.79 | loop fusion | bytes 75497472 | tf_op jit(solution)/shard_map/while/body/eval_jaxpr/slice | solution.py:89
  902.2 19.3 fusion.6
  965.8 18.7 convolution_bitcast_fusion
  984.5 15.4 select_maximum_fusion
  1005.7 601.5 %while.3 = (s32[]{:T(128)}, bf16[1,64,98,514]{1,3,2,0:T(8,128)(2,1)}, s32[32,4]{0,1:T(4,128)S(1)}, bf16[32,64,34,34]{1,0,3,2:T(8,128)(2,1)}, s32[]{:T(128)}, /*index=5*/s32[]{:T(128)}) while((s32[]{:T(128)}, bf16[1,64,98,514]{1,3,2,0:T(8,128)(2,1)}, s32[32,4]{0,1:T(4,128)S(1)}, bf16[32,64,34,34]{1,0,3,2:T(8,128)(2,1)}, s32[]{:T(128)}, ...), condition=%wide.while_cond.1, body=%wide.while_body.1.sunk | while | flops 2 | bytes 887949 | solution.py:68
  1027.9 15.3 dynamic-update-slice.43
  1065.5 15.3 dynamic-update-slice.43
  1103.1 15.3 dynamic-update-slice.43
  1140.7 15.3 dynamic-update-slice.43
  1159.5 15.3 dynamic-update-slice.43
  1178.3 15.3 dynamic-update-slice.43
  1197.1 15.3 dynamic-update-slice.43
  1215.9 15.3 dynamic-update-slice.43
  1234.7 15.3 dynamic-update-slice.43
  1253.5 15.3 dynamic-update-slice.43
  1272.3 15.3 dynamic-update-slice.43
  1291.1 15.3 dynamic-update-slice.43
  1309.9 15.3 dynamic-update-slice.43
  1328.7 15.3 dynamic-update-slice.43
  1347.5 15.3 dynamic-update-slice.43
  1366.3 15.3 dynamic-update-slice.43
  1385.1 15.3 dynamic-update-slice.43
  1403.9 15.3 dynamic-update-slice.43
  1422.7 15.3 dynamic-update-slice.43
  1441.5 15.3 dynamic-update-slice.43
  1479.0 15.3 dynamic-update-slice.43
  1516.6 15.3 dynamic-update-slice.43
  1554.2 15.3 dynamic-update-slice.43
  1591.8 15.3 dynamic-update-slice.43
  1615.4 23.8 %fusion.19 = (bf16[32,64,32,32]{1,0,3,2:T(8,128)(2,1)}, bf16[32,64,32,32]{1,0,3,2:T(8,128)(2,1)}, bf16[32,64,32,32]{1,0,3,2:T(8,128)(2,1)}, bf16[32,64,32,32]{1,...) fusion(bf16[32,64,34,34]{1,0,3,2:T(8,128)(2,1)S(1)} %bitcast.112), kind=kLoop, calls=%fused_computation.78 | loop fusion | bytes 75497472 | tf_op jit(solution)/shard_map/while/body/eval_jaxpr/slice | solution.py:89
  1755.3 16.9 convolution_bitcast_fusion.1
  1772.2 17.9 fusion.7
  1842.9 78.9 %all-reduce.7.cloned.1.call-done = (f32[576,64]{0,1:T(8,128)}, f32[576,64]{0,1:T(8,128)}) async-done(((f32[576,64]{0,1:T(8,128)}, f32[576,64]{0,1:T(8,128)}), (f32[576,64]{0,1:T(8,128)}, f32[576,64]{0,1:T(8,128)})) %all-reduce.7.cloned.1.call-update) | async-done | bytes 294928 | tf_op jit(solution)/shard_map/psum | solution.py:168
  (421 shorter events, 864.5 us)
Async XLA Ops:
  7.2 895.1 %copy-start = (bf16[9,64,64]{2,1,0:T(8,128)(2,1)S(1)}, bf16[9,64,64]{2,1,0:T(8,128)(2,1)}, u32[]{:S(2)}) copy-start(bf16[9,64,64]{2,1,0:T(8,128)(2,1)} %param.11) | copy-start | bytes 221188
  7.2 1914.7 %all-reduce.7.cloned.1.call-start = ((), (), s32[]{:S(2)}) async-start(), calls=%async_computation | async-start | bytes 655360 | tf_op jit(solution)/shard_map/psum | solution.py:168
  48.2 33.2 %copy-start.26 = (s32[1,32]{1,0:T(1,128)S(1)}, s32[1,32]{1,0:T(1,128)}, u32[]{:S(2)}) copy-start(s32[1,32]{1,0:T(1,128)} %param.13) | copy-start | bytes 388
  75.9 57.5 %collective-permute-start = (bf16[1,64,1,512]{1,3,2,0:T(8,128)(2,1)S(1)}, bf16[1,64,1,512]{1,3,2,0:T(8,128)(2,1)S(1)}, u32[]{:S(2)}, u32[]{:S(2)}) collective-permute-start(bf16[1,64,1,512]{1,3,2,0:T(8,128)(2,1)S(1)} %get-tuple-element.118), channel_id=1, source_target_pairs={{0,1},{1,2},{2,3},{3,4},{4,5},{5,6},{6,7},{7,8},{8,9},{9,10},{10,1... | collective-permute-start | bytes 196616 | tf_op jit(solution)/shard_map/ppermute | solution.py:19
  79.9 53.5 %collective-permute-start.1 = (bf16[1,64,1,512]{1,3,2,0:T(8,128)(2,1)S(1)}, bf16[1,64,1,512]{1,3,2,0:T(8,128)(2,1)S(1)}, u32[]{:S(2)}, u32[]{:S(2)}) collective-permute-start(bf16[1,64,1,512]{1,3,2,0:T(8,128)(2,1)S(1)} %get-tuple-element.119), channel_id=1, source_target_pairs={{1,0},{2,1},{3,2},{4,3},{5,4},{6,5},{7,6},{8,7},{9,8},{10,9},{11,1... | collective-permute-start | bytes 196616 | tf_op jit(solution)/shard_map/ppermute | solution.py:20
  756.1 6.5 copy-start.20
  876.3 5.2 copy-start.18
  876.3 7.8 copy-start.16
  881.5 5.2 copy-start.14
  884.1 5.2 copy-start.12
  886.7 5.2 copy-start.10
  889.3 5.2 copy-start.8
  891.9 5.2 copy-start.6
  894.4 5.3 copy-start.4
  902.2 22.8 %copy-start.24 = (s32[32]{0:T(128)S(1)}, s32[32]{0:T(128)}, u32[]{:S(2)}) copy-start(s32[32]{0:T(128)} %fusion.9) | copy-start | bytes 388
  948.2 17.5 copy-start.3
  955.9 4.5 copy-start.2
  960.5 24.0 %collective-permute-start.2 = (bf16[1,64,1,512]{1,3,2,0:T(8,128)(2,1)S(1)}, bf16[1,64,1,512]{1,3,2,0:T(8,128)(2,1)S(1)}, u32[]{:S(2)}, u32[]{:S(2)}) collective-permute-start(bf16[1,64,1,512]{1,3,2,0:T(8,128)(2,1)S(1)} %get-tuple-element.116), channel_id=1, source_target_pairs={{0,1},{1,2},{2,3},{3,4},{4,5},{5,6},{6,7},{7,8},{8,9},{9,10},{10,1... | collective-permute-start | bytes 196616 | tf_op jit(solution)/shard_map/ppermute | solution.py:19
  964.5 20.0 %collective-permute-start.3 = (bf16[1,64,1,512]{1,3,2,0:T(8,128)(2,1)S(1)}, bf16[1,64,1,512]{1,3,2,0:T(8,128)(2,1)S(1)}, u32[]{:S(2)}, u32[]{:S(2)}) collective-permute-start(bf16[1,64,1,512]{1,3,2,0:T(8,128)(2,1)S(1)} %get-tuple-element.117), channel_id=1, source_target_pairs={{1,0},{2,1},{3,2},{4,3},{5,4},{6,5},{7,6},{8,7},{9,8},{10,9},{11,1... | collective-permute-start | bytes 196616 | tf_op jit(solution)/shard_map/ppermute | solution.py:20
  999.9 5.8 copy-start.21
  1727.3 5.2 copy-start.19
  1727.3 7.8 copy-start.17
  1732.5 5.2 copy-start.15
  1735.1 5.2 copy-start.13
  1737.7 5.2 copy-start.11
  1740.3 5.2 copy-start.9
  1742.9 5.2 copy-start.7
  1745.4 5.3 copy-start.5
  1748.0 5.4 slice-start
  1750.7 4.6 slice-start.1
  1755.3 16.9 copy-start.22
  1755.3 16.9 copy-start.23
  1772.2 21.5 %copy-start.25 = (s32[32]{0:T(128)S(1)}, s32[32]{0:T(128)}, u32[]{:S(2)}) copy-start(s32[32]{0:T(128)} %fusion.9) | copy-start | bytes 388
  1828.5 97.0 %copy-start.1 = (bf16[9,64,64]{2,1,0:T(8,128)(2,1)S(1)}, bf16[9,64,64]{2,1,0:T(8,128)(2,1)}, u32[]{:S(2)}) copy-start(bf16[9,64,64]{2,1,0:T(8,128)(2,1)} %param.11) | copy-start | bytes 221188
Sparse Core Ops, SparseCore 0:
  1772.3 149.5 all-reduce.6
where the time goes:
time: 1970 us; the launch traced here: 1930 us
  local copies, waits for them, and re-layouts  1690 us (86%)
  waiting for transfers between devices  79 us (4%)
  matrix products  72.7 us (4%)
  other arithmetic  60.7 us (3%)
    gather x320, local copies, waits for them, and re-layouts  1200 us
    reshape x18, local copies, waits for them, and re-layouts, shifted_stack(): pieces.append(shifted.reshape(slot_total, channels, tile_side * tile_side))  176 us
    unnamed x81, local copies, waits for them, and re-layouts  119 us
    psum x1, waiting for transfers between devices, shards(): lax.psum((first_part, second_part), ('tm', 'space'))  78.9 us
    slice x2, local copies, waits for them, and re-layouts, shifted_stack(): grid_view[:, :, 1 - step_row:1 - step_row + tile_side, 1 - step_col:1 - s...  47.5 us
    scatter x5, local copies, waits for them, and re-layouts, fill_hour(): return canvas.at[hour_ids].set(hour_values, mode='promise_in_bounds')  46.5 us
  transfers between devices with their start and end apart: 5, of which 1 were waited for; matrix products, arithmetic and copies ran while one was open for 7% of the time, Pallas kernels for 0%

commit v1 on v0

v1 whole, which is shorter than its diff:
```python
import math

import jax
import jax.numpy as jnp
from jax import lax
from jax.experimental import pallas as pl
from jax.experimental.pallas import tpu as pltpu
from jax.sharding import PartitionSpec as P

F32 = jnp.float32
BF = jnp.bfloat16
C = 64
TS = 32
ROWS = 96
WIDTH = 512
STRIP = 16
STRIPS = ROWS // STRIP
PAIR = 2 * C
PAIRS = ROWS // 2
TM = 8
SPACE = 16
CHUNK = 3 * C // TM
NT = (((1,), (1,)), ((), ()))
MESH = pl.DeviceIdType.MESH
ORDER = (1, 0, -1)


def al(x, m=C):
    return x if isinstance(x, int) else pl.multiple_of(x, m)


def shift_right(x):
    lane = lax.broadcasted_iota(jnp.int32, (x.shape[0], 128), 1)
    out, carry = [], None
    for j in range(x.shape[1] // 128):
        r = pltpu.roll(x[:, j * 128 : (j + 1) * 128], 1, 1)
        out.append(jnp.where(lane == 0, jnp.zeros_like(r) if carry is None else carry, r))
        carry = r
    return jnp.concatenate(out, axis=1)


def shift_left(x):
    lane = lax.broadcasted_iota(jnp.int32, (x.shape[0], 128), 1)
    out, carry = [], None
    for j in reversed(range(x.shape[1] // 128)):
        r = pltpu.roll(x[:, j * 128 : (j + 1) * 128], 127, 1)
        out.append(jnp.where(lane == 127, jnp.zeros_like(r) if carry is None else carry, r))
        carry = r
    return jnp.concatenate(out[::-1], axis=1)


def build_weight(w_ref, out_ref):
    zero = jnp.zeros((C, C), F32)
    rows = []
    for q in range(4):
        cols = []
        for dc in ORDER:
            for t in range(2):
                dr = t + 1 - q
                cols.append(w_ref[(dr + 1) * 3 + dc + 1].astype(F32) if abs(dr) <= 1 else zero)
        rows.append(jnp.concatenate(cols, axis=1))
    out_ref[...] = jnp.concatenate(rows, axis=0).T.astype(BF)


def build_mask(mask_ref, out_ref):
    first = lax.axis_index("space") * (ROWS // TS)
    count, cols = mask_ref.shape
    pick = lax.broadcasted_iota(jnp.int32, (8, count), 0) + first
    pick = (pick == lax.broadcasted_iota(jnp.int32, (8, count), 1)).astype(F32).astype(BF)
    own = jnp.dot(pick, mask_ref[...].astype(F32).astype(BF), preferred_element_type=F32)
    spread = lax.broadcasted_iota(jnp.int32, (cols, WIDTH), 1) >> 5
    spread = (spread == lax.broadcasted_iota(jnp.int32, (cols, WIDTH), 0)).astype(F32).astype(BF)
    out_ref[...] = jnp.dot(own.astype(BF), spread, preferred_element_type=F32)


def conv_pair(weight, src_ref, base):
    part = jnp.dot(weight, src_ref[pl.ds(al(base), 2 * PAIR), :], preferred_element_type=F32)
    return shift_right(part[:PAIR]) + part[PAIR : 2 * PAIR] + shift_left(part[2 * PAIR :])


def grad_pair(own_ref, own_base, src_ref, base):
    own = own_ref[pl.ds(al(own_base), PAIR), :]
    own = jnp.concatenate([shift_right(own), own, shift_left(own)], axis=0)
    return lax.dot_general(own, src_ref[pl.ds(al(base), 2 * PAIR), :], NT, preferred_element_type=F32)


def main_kernel(
    cot_hbm, pre_hbm, feat_hbm, w2_ref, mask_ref, p_hbm, total_ref,
    cot_in, pre_in, feat_in, g, kept, inp, pgrad, weight, cells, acc2, acc1,
    part, gathered, scattered, summed,
    in_sem, out_sem, halo_send, halo_recv, rs_send, rs_recv, sp_send, sp_recv, ag_send, ag_recv,
):
    tm = lax.axis_index("tm")
    sp = lax.axis_index("space")
    up, down = lax.rem(sp + SPACE - 1, SPACE), lax.rem(sp + 1, SPACE)
    sources = ((cot_hbm, cot_in), (pre_hbm, pre_in), (feat_hbm, feat_in))

    def fetch(a, s):
        src, dst = sources[a]
        rows = pl.ds(al(s * STRIP, STRIP), STRIP)
        return pltpu.make_async_copy(src.at[:, rows, :], dst.at[:, rows, :], in_sem.at[a, s])

    for s in (0, STRIPS - 1):
        fetch(0, s).start()
        fetch(1, s).start()
    for s in range(1, STRIPS - 1):
        fetch(0, s).start()
        fetch(1, s).start()
    for s in range(STRIPS):
        fetch(2, s).start()

    barrier = pltpu.get_barrier_semaphore()
    for j in range(1, TM):
        pl.semaphore_signal(barrier, inc=1, device_id=(lax.rem(tm + j, TM), sp), device_id_type=MESH)
    for j in range(1, SPACE):
        pl.semaphore_signal(barrier, inc=1, device_id=(tm, lax.rem(sp + j, SPACE)), device_id_type=MESH)

    build_mask(mask_ref, cells)
    build_weight(w2_ref, weight)
    acc2[...] = jnp.zeros_like(acc2)
    acc1[...] = jnp.zeros_like(acc1)

    def strip_of(ref, s):
        mask = cells[pl.ds(s // 2, 1), :].astype(BF)
        return ref[:, pl.ds(al(s * STRIP, STRIP), STRIP), :], mask[None]

    def put(ref, first_row, s, x):
        x = jnp.transpose(x, (1, 0, 2)).reshape(STRIP * C, WIDTH)
        ref[pl.ds(al((s * STRIP + first_row) * C), STRIP * C), :] = x

    def load_cot_pre(s):
        x, mask = strip_of(cot_in, s)
        put(g, 2, s, x * mask)
        x, mask = strip_of(pre_in, s)
        put(kept, 1, s, jnp.maximum(x, jnp.zeros((), BF)) * mask)

    def load_feat(s):
        x, mask = strip_of(feat_in, s)
        put(inp, 0, s, x * mask)

    for s in (0, STRIPS - 1):
        fetch(0, s).wait()
        fetch(1, s).wait()
        load_cot_pre(s)

    pl.semaphore_wait(barrier, TM + SPACE - 2)

    def halo(i, ref, src_row, dst_row, count, to):
        return pltpu.make_async_remote_copy(
            src_ref=ref.at[pl.ds(src_row * C, count * C), :],
            dst_ref=ref.at[pl.ds(dst_row * C, count * C), :],
            send_sem=halo_send.at[i],
            recv_sem=halo_recv.at[i],
            device_id=(tm, to),
            device_id_type=MESH,
        )

    halos = (
        halo(0, g, 2, ROWS + 2, 2, up),
        halo(1, g, ROWS, 0, 2, down),
        halo(2, kept, 1, ROWS + 1, 1, up),
        halo(3, kept, ROWS, 0, 1, down),
    )
    for h in halos:
        h.start()

    fetch(0, 1).wait()
    fetch(1, 1).wait()
    load_cot_pre(1)

    def second_conv(p):
        base = p * PAIR
        out = conv_pair(weight[...], g, base).astype(BF)
        positive = kept[pl.ds(al(base), PAIR), :] > 0
        pgrad[pl.ds(al(base), PAIR), :] = jnp.where(positive, out, jnp.zeros((), BF))

    def second_grad(p):
        base = p * PAIR + C
        acc2[...] += grad_pair(kept, base, g, base)

    def pass1(s):
        for q in range(1, STRIP // 2 + 1):
            second_conv(s * (STRIP // 2) + q)
            second_grad(s * (STRIP // 2) + q)

    def body1(s, carry):
        fetch(0, s + 2).wait()
        fetch(1, s + 2).wait()
        load_cot_pre(s + 2)
        pass1(s)
        return carry

    lax.fori_loop(0, STRIPS - 3, body1, 0)

    def body1_late(s, carry):
        pass1(s)
        return carry

    lax.fori_loop(STRIPS - 3, STRIPS - 1, body1_late, 0)

    for h in halos:
        h.wait()

    @pl.when(sp == 0)
    def _():
        g[pl.ds(0, 2 * C), :] = jnp.zeros((2 * C, WIDTH), BF)
        kept[pl.ds(0, C), :] = jnp.zeros((C, WIDTH), BF)

    @pl.when(sp == SPACE - 1)
    def _():
        g[pl.ds((ROWS + 2) * C, 2 * C), :] = jnp.zeros((2 * C, WIDTH), BF)
        kept[pl.ds((ROWS + 1) * C, C), :] = jnp.zeros((C, WIDTH), BF)

    for q in range(PAIRS - 7, PAIRS):
        second_conv(q)
        second_grad(q)
    for q in (0, PAIRS):
        second_conv(q)
    second_grad(0)

    save = pltpu.make_async_copy(pgrad, p_hbm, out_sem)
    save.start()

    fetch(2, 0).wait()
    load_feat(0)

    def pass2(s):
        for q in range(STRIP // 2):
            base = (s * (STRIP // 2) + q) * PAIR
            acc1[...] += grad_pair(inp, base, pgrad, base)

    def body2(s, carry):
        fetch(2, s + 1).wait()
        load_feat(s + 1)
        pass2(s)
        return carry

    lax.fori_loop(0, STRIPS - 1, body2, 0)
    pass2(STRIPS - 1)

    for s in range(3):
        both = []
        for acc in (acc1, acc2):
            top = acc[pl.ds(s * PAIR, C), :][:, : 3 * C]
            both.append(top + acc[pl.ds(s * PAIR + C, C), :][:, C:])
        both = jnp.concatenate(both, axis=1)
        for r in range(0, C, 8):
            row = s * C + r
            part[row // CHUNK, pl.ds(row % CHUNK, 8), :] = both[r : r + 8]

    def exchange(src, dst, send, recv, slot, to):
        return pltpu.make_async_remote_copy(
            src_ref=src, dst_ref=dst, send_sem=send.at[slot], recv_sem=recv.at[slot],
            device_id=to, device_id_type=MESH,
        )

    copies = []
    for j in range(1, TM):
        t = lax.rem(tm + j, TM)
        copies.append(exchange(part.at[t], scattered.at[j - 1], rs_send, rs_recv, j - 1, (t, sp)))
        copies[-1].start()
    for c in copies:
        c.wait()
    mine = part[tm]
    for j in range(TM - 1):
        mine = mine + scattered[j]
    summed[...] = mine

    peers = [lax.rem(sp + j, SPACE) for j in range(1, SPACE)]
    sends = [
        pltpu.make_async_remote_copy(
            src_ref=summed, dst_ref=gathered.at[sp], send_sem=sp_send.at[j], recv_sem=sp_recv.at[sp],
            device_id=(tm, to), device_id_type=MESH,
        )
        for j, to in enumerate(peers)
    ]
    for c in sends:
        c.start()
    gathered[sp] = mine
    for c in sends:
        c.wait_send()
    for peer in peers:
        pltpu.make_async_remote_copy(
            src_ref=summed, dst_ref=gathered.at[peer], send_sem=sp_send.at[0], recv_sem=sp_recv.at[peer],
            device_id=(tm, peer), device_id_type=MESH,
        ).wait_recv()
    whole = gathered[0]
    for j in range(1, SPACE):
        whole = whole + gathered[j]
    total_ref[tm] = whole

    peers = [lax.rem(tm + j, TM) for j in range(1, TM)]
    sends = [
        pltpu.make_async_remote_copy(
            src_ref=total_ref.at[tm], dst_ref=total_ref.at[tm], send_sem=ag_send.at[j], recv_sem=ag_recv.at[tm],
            device_id=(to, sp), device_id_type=MESH,
        )
        for j, to in enumerate(peers)
    ]
    for c in sends:
        c.start()
    for c in sends:
        c.wait_send()
    for peer in peers:
        pltpu.make_async_remote_copy(
            src_ref=total_ref.at[tm], dst_ref=total_ref.at[peer], send_sem=ag_send.at[0], recv_sem=ag_recv.at[peer],
            device_id=(peer, sp), device_id_type=MESH,
        ).wait_recv()
    save.wait()


def last_kernel(
    p_hbm, w1_ref, mask_ref, total_ref, out_hbm, first_ref, second_ref,
    pgrad, rows, outs, weight, cells, in_sem, out_sem,
):
    def fetch(s):
        start, size = (0, (STRIP + 2) * C) if s == 0 else ((s * STRIP + 2) * C, STRIP * C)
        return pltpu.make_async_copy(p_hbm.at[pl.ds(start, size), :], pgrad.at[pl.ds(start, size), :], in_sem.at[s])

    for s in range(STRIPS):
        fetch(s).start()
    build_mask(mask_ref, cells)
    build_weight(w1_ref, weight)

    def store(s):
        r = pl.ds(al(s * STRIP, STRIP), STRIP)
        return pltpu.make_async_copy(outs.at[:, r, :], out_hbm.at[:, r, :], out_sem.at[s])

    for s in range(STRIPS):
        fetch(s).wait()
        mask = cells[pl.ds(s // 2, 1), :]
        for q in range(STRIP // 2):
            base = (s * (STRIP // 2) + q) * PAIR
            rows[pl.ds(base, PAIR), :] = (conv_pair(weight[...], pgrad, base) * mask).astype(BF)
        x = rows[pl.ds(s * STRIP * C, STRIP * C), :].reshape(STRIP, C, WIDTH)
        outs[:, pl.ds(s * STRIP, STRIP), :] = jnp.transpose(x, (1, 0, 2))
        store(s).start()

    scale = 1.0 / math.sqrt(TM * ROWS * SPACE * WIDTH)
    grid = total_ref[...].T * scale
    for n, ref in enumerate((first_ref, second_ref)):
        for q in range(3):
            row = (n * 3 + q) * C
            for s in range(3):
                ref[(2 - q) * 3 + s] = grid[row : row + C, s * C : (s + 1) * C]
    for s in range(STRIPS):
        store(s).wait()


def block(features, pre_act, cotangent, first_weight, second_weight, tile_mask, tile_list):
    vmem = pl.BlockSpec(memory_space=pltpu.VMEM)
    hbm = pl.BlockSpec(memory_space=pl.ANY)
    shape = (C, ROWS, WIDTH)
    mask = tile_mask[0]
    chunk = (CHUNK, 6 * C)
    dma = pltpu.SemaphoreType.DMA
    pgrad, total = pl.pallas_call(
        main_kernel,
        out_shape=(
            jax.ShapeDtypeStruct(((ROWS + 2) * C, WIDTH), BF),
            jax.ShapeDtypeStruct((TM,) + chunk, F32),
        ),
        in_specs=[hbm, hbm, hbm, vmem, vmem],
        out_specs=(hbm, vmem),
        scratch_shapes=[
            pltpu.VMEM(shape, BF),
            pltpu.VMEM(shape, BF),
            pltpu.VMEM(shape, BF),
            pltpu.VMEM(((ROWS + 4) * C, WIDTH), BF),
            pltpu.VMEM(((ROWS + 2) * C, WIDTH), BF),
            pltpu.VMEM((ROWS * C, WIDTH), BF),
            pltpu.VMEM(((ROWS + 2) * C, WIDTH), BF),
            pltpu.VMEM((3 * PAIR, 2 * PAIR), BF),
            pltpu.VMEM((8, WIDTH), F32),
            pltpu.VMEM((3 * PAIR, 2 * PAIR), F32),
            pltpu.VMEM((3 * PAIR, 2 * PAIR), F32),
            pltpu.VMEM((TM,) + chunk, F32),
            pltpu.VMEM((SPACE,) + chunk, F32),
            pltpu.VMEM((TM - 1,) + chunk, F32),
            pltpu.VMEM(chunk, F32),
            dma((3, STRIPS)),
            dma(()),
            dma((4,)),
            dma((4,)),
            dma((TM - 1,)),
            dma((TM - 1,)),
            dma((SPACE,)),
            dma((SPACE,)),
            dma((TM,)),
            dma((TM,)),
        ],
        compiler_params=pltpu.CompilerParams(
            collective_id=0, has_side_effects=True, vmem_limit_bytes=60 * 2**20
        ),
        name="grads",
    )(cotangent[0], pre_act[0], features[0], second_weight, mask)
    grad, first, second = pl.pallas_call(
        last_kernel,
        out_shape=(
            jax.ShapeDtypeStruct(shape, BF),
            jax.ShapeDtypeStruct((9, C, C), F32),
            jax.ShapeDtypeStruct((9, C, C), F32),
        ),
        in_specs=[hbm, vmem, vmem, vmem],
        out_specs=(hbm, vmem, vmem),
        scratch_shapes=[
            pltpu.VMEM(((ROWS + 2) * C, WIDTH), BF),
            pltpu.VMEM((ROWS * C, WIDTH), BF),
            pltpu.VMEM(shape, BF),
            pltpu.VMEM((3 * PAIR, 2 * PAIR), BF),
            pltpu.VMEM((8, WIDTH), F32),
            dma((STRIPS,)),
            dma((STRIPS,)),
        ],
        compiler_params=pltpu.CompilerParams(vmem_limit_bytes=60 * 2**20),
        name="input_grad",
    )(pgrad, first_weight, mask, total.reshape(TM * CHUNK, 6 * C))
    return grad[None], first, second


def solution(mesh):
    return jax.shard_map(
        block,
        mesh=mesh,
        in_specs=(
            P("tm", None, "space", None),
            P("tm", None, "space", None),
            P("tm", None, "space", None),
            P(),
            P(),
            P("tm", None, None),
            P("tm", "space"),
        ),
        out_specs=(P("tm", None, "space", None), P(), P()),
        check_vma=False,
    )
```

time: 1970 us -> 69.8 us (0.04); the launches traced: 1930 us -> 69.3 us
  local copies, waits for them, and re-layouts: 1690 us -> 1.38 us
  waiting for transfers between devices: 79 us -> 0 us
  matrix products: 72.7 us -> 0 us
  Pallas kernels: 0 us -> 67.1 us
  other arithmetic: 60.7 us -> 0 us
    gather x324 -> x0, local copies, waits for them, and re-layouts: 1220 us -> none
    reshape x20 -> x0, local copies, waits for them, and re-layouts: 189 us -> none  [the longest x18 176 us: shifted_stack(): pieces.append(shifted.reshape(slot_total, channels, tile_side * tile_side))]
    unnamed x81 -> x1, local copies, waits for them, and re-layouts: 119 us -> 1.38 us
    psum x1 -> x0, waiting for transfers between devices: 78.9 us -> none  [shards(): lax.psum((first_part, second_part), ('tm', 'space'))]
    dot_general x4 -> x0, matrix products: 72.7 us -> none  [the longest x1 19.3 us: second_layer(): jnp.einsum('ik,skq->siq', weight_rows, stacked, preferred_element_type=jn...]
    pallas_call x0 -> x2, Pallas kernels: none -> 67.1 us  [the longest x1 52.7 us: block(): pl.pallas_call(main_kernel, out_shape=(jax.ShapeDtypeStruct(((ROWS + 2) *...]
    slice x6 -> x0, local copies, waits for them, and re-layouts: 52 us -> none  [the longest x2 47.5 us: shifted_stack(): grid_view[:, :, 1 - step_row:1 - step_row + tile_side, 1 - step_col:1 - s...]
    scatter x5 -> x0, local copies, waits for them, and re-layouts: 46.5 us -> none  [fill_hour(): return canvas.at[hour_ids].set(hour_values, mode='promise_in_bounds')]
  transfers between devices with their start and end apart: 5 -> 0, of which waited for: 1 -> 0; matrix products, arithmetic and copies ran while one was open for 7% -> 0% of each run, Pallas kernels for 0% -> 0%
where the time goes in v1:
time: 69.8 us; the launch traced here: 69.3 us
  Pallas kernels  67.1 us (96%)
  local copies, waits for them, and re-layouts  1.38 us (2%)
  between operations  0.8 us (1%)
    pallas_call x1, Pallas kernels, block(): pl.pallas_call(main_kernel, out_shape=(jax.ShapeDtypeStruct(((ROWS + 2) *...  52.7 us
    pallas_call x1, Pallas kernels, block(): pl.pallas_call(last_kernel, out_shape=(jax.ShapeDtypeStruct(shape, BF), j...  14.4 us

profile of v1, /device:TPU:1, one launch (start us, length us, event | category | flops | bytes accessed | tf_op | source)
XLA Modules:
  0.0 69.3 jit_solution(16217648473935950892)
XLA Ops:
  0.6 1.4 %copy.9 = s32[1,48,16]{2,1,0:T(8,128)} copy(s32[1,48,16]{1,2,0:T(8,128)} %param.12) | data formatting | bytes 6144 | tf_op args[5]
  2.0 52.7 %grads.1 = (bf16[6272,512]{1,0:T(8,128)(2,1)}, f32[8,24,384]{2,1,0:T(8,128)}) custom-call(bf16[64,96,512]{2,1,0:T(8,128)(2,1)} %bitcast.6, bf16[64,96,512]{2,1,0:T(8,128)(2,1)} %bitcast.7, bf16[64,96,512]{2,1,0:T(8,128)(2,1)} %bitcast.8, bf16[9,64,64]{2,1,0:T(8,128)(2,1)} %w2_ref.1, s32[48,16]{1,0:T(8,128)} %bitcast.10), custom_call_target="tpu_custom_call" | custom-call | tf_op jit(solution)/shard_map/grads/pallas_call | solution.py:357
  54.7 14.4 %input_grad.1 = (bf16[64,96,512]{2,1,0:T(8,128)(2,1)}, f32[9,64,64]{2,1,0:T(8,128)}, f32[9,64,64]{2,1,0:T(8,128)}) custom-call(bf16[6272,512]{1,0:T(8,128)(2,1)} %get-tuple-element.8.p_hbm, bf16[9,64,64]{2,1,0:T(8,128)(2,1)} %w1_ref.1, s32[48,16]{1,0:T(8,128)} %bitcast.11, f32[192,384]{1,0:T(8,128)} %bitcast.9), custom_call_target="tpu_custom_call" | custom-call | tf_op jit(solution)/shard_map/input_grad/pallas_call | solution.py:397

commit v2 on v1

v2 whole, which is shorter than its diff:
```python
import math

import jax
import jax.numpy as jnp
from jax import lax
from jax.experimental import pallas as pl
from jax.experimental.pallas import tpu as pltpu
from jax.sharding import PartitionSpec as P

F32 = jnp.float32
BF = jnp.bfloat16
C = 64
TS = 32
ROWS = 96
WIDTH = 512
STRIP = 16
STRIPS = ROWS // STRIP
PAIR = 2 * C
PAIRS = ROWS // 2
TM = 8
SPACE = 16
HALF = STRIP // 2
LANES = 128
GRAD_ROWS = 9 * C // 2
USED = 2 * GRAD_ROWS // TM
CHUNK = 80
RING = 4
PARTS = 8
NT = (((1,), (1,)), ((), ()))
MESH = pl.DeviceIdType.MESH
ORDER = (1, 0, -1)


def al(x, m=C):
    return x if isinstance(x, int) else pl.multiple_of(x, m)


def shift_right(x):
    lane = lax.broadcasted_iota(jnp.int32, (x.shape[0], 128), 1)
    out, carry = [], None
    for j in range(x.shape[1] // 128):
        r = pltpu.roll(x[:, j * 128 : (j + 1) * 128], 1, 1)
        out.append(jnp.where(lane == 0, jnp.zeros_like(r) if carry is None else carry, r))
        carry = r
    return jnp.concatenate(out, axis=1)


def shift_left(x):
    lane = lax.broadcasted_iota(jnp.int32, (x.shape[0], 128), 1)
    out, carry = [], None
    for j in reversed(range(x.shape[1] // 128)):
        r = pltpu.roll(x[:, j * 128 : (j + 1) * 128], 127, 1)
        out.append(jnp.where(lane == 127, jnp.zeros_like(r) if carry is None else carry, r))
        carry = r
    return jnp.concatenate(out[::-1], axis=1)


def build_weight(w_ref, out_ref):
    zero = jnp.zeros((C, C), F32)
    rows = []
    for q in range(4):
        cols = []
        for dc in ORDER:
            for t in range(2):
                dr = t + 1 - q
                cols.append(w_ref[(dr + 1) * 3 + dc + 1].astype(F32) if abs(dr) <= 1 else zero)
        rows.append(jnp.concatenate(cols, axis=1))
    out_ref[...] = jnp.concatenate(rows, axis=0).T.astype(BF)


def build_mask(mask_ref, out_ref):
    first = lax.axis_index("space") * (ROWS // TS)
    cols, count = mask_ref.shape
    pick = lax.broadcasted_iota(jnp.int32, (8, count), 0) + first
    pick = (pick == lax.broadcasted_iota(jnp.int32, (8, count), 1)).astype(F32).astype(BF)
    own = lax.dot_general(pick, mask_ref[...].astype(F32).astype(BF), NT, preferred_element_type=F32)
    spread = lax.broadcasted_iota(jnp.int32, (cols, WIDTH), 1) >> 5
    spread = (spread == lax.broadcasted_iota(jnp.int32, (cols, WIDTH), 0)).astype(F32).astype(BF)
    out_ref[...] = jnp.dot(own.astype(BF), spread, preferred_element_type=F32)


def conv_pair(weight, src_ref, base):
    part = jnp.dot(weight, src_ref[pl.ds(al(base), 2 * PAIR), :], preferred_element_type=F32)
    return shift_right(part[:PAIR]) + part[PAIR : 2 * PAIR] + shift_left(part[2 * PAIR :])


def grad_pair(own_ref, own_base, src_ref, base):
    own = own_ref[pl.ds(al(own_base), PAIR), :]
    own = jnp.concatenate([shift_right(own), own, shift_left(own)], axis=0)
    return lax.dot_general(own, src_ref[pl.ds(al(base), 2 * PAIR), :], NT, preferred_element_type=F32)


def main_kernel(
    cot_hbm, pre_hbm, feat_hbm, w2_ref, w1_ref, mask_ref, out_hbm, total_ref,
    cot_in, pre_in, feat_in, g, kept, inp, pgrad, weight2, weight1, cells, acc2, acc1,
    flat, part, scattered, near, far,
    in_sem, out_sem, halo_send, halo_recv, rs_send, rs_recv, y_send, y_recv, x_send, x_recv, ag_send, ag_recv,
):
    tm = lax.axis_index("tm")
    sp = lax.axis_index("space")
    up, down = lax.rem(sp + SPACE - 1, SPACE), lax.rem(sp + 1, SPACE)
    x, y = sp // RING, lax.rem(sp, RING)

    def y_peer(j):
        return x * RING + lax.rem(y + j, RING)

    def x_peer(j):
        return lax.rem(x + j, RING) * RING + y

    sources = ((cot_hbm, cot_in), (pre_hbm, pre_in), (feat_hbm, feat_in))

    def fetch(a, s):
        src, dst = sources[a]
        rows = pl.ds(al(s * STRIP, STRIP), STRIP)
        return pltpu.make_async_copy(src.at[:, rows, :], dst.at[:, rows, :], in_sem.at[a, s])

    for s in (0, 1, STRIPS - 1) + tuple(range(2, STRIPS - 1)):
        fetch(0, s).start()
        fetch(1, s).start()
    for s in range(STRIPS):
        fetch(2, s).start()

    barrier = pltpu.get_barrier_semaphore()
    for j in range(1, TM):
        pl.semaphore_signal(barrier, inc=1, device_id=(lax.rem(tm + j, TM), sp), device_id_type=MESH)
    for j in range(1, RING):
        pl.semaphore_signal(barrier, inc=1, device_id=(tm, y_peer(j)), device_id_type=MESH)
        pl.semaphore_signal(barrier, inc=1, device_id=(tm, x_peer(j)), device_id_type=MESH)
    for to in (up, down):
        pl.semaphore_signal(barrier, inc=1, device_id=(tm, to), device_id_type=MESH)

    build_mask(mask_ref, cells)
    build_weight(w2_ref, weight2)
    acc2[...] = jnp.zeros_like(acc2)
    acc1[...] = jnp.zeros_like(acc1)

    def strip_of(ref, s):
        mask = cells[pl.ds(s // 2, 1), :].astype(BF)
        return ref[:, pl.ds(al(s * STRIP, STRIP), STRIP), :], mask[None]

    def put(ref, first_row, s, x):
        x = jnp.transpose(x, (1, 0, 2)).reshape(STRIP * C, WIDTH)
        ref[pl.ds(al((s * STRIP + first_row) * C), STRIP * C), :] = x

    def load_cot_pre(s):
        v, mask = strip_of(cot_in, s)
        put(g, 2, s, v * mask)
        v, mask = strip_of(pre_in, s)
        put(kept, 1, s, jnp.maximum(v, jnp.zeros((), BF)) * mask)

    def load_feat(s):
        v, mask = strip_of(feat_in, s)
        put(inp, 0, s, v * mask)

    def halo(i, ref, src_row, dst_row, count, to):
        return pltpu.make_async_remote_copy(
            src_ref=ref.at[pl.ds(src_row * C, count * C), :],
            dst_ref=ref.at[pl.ds(dst_row * C, count * C), :],
            send_sem=halo_send.at[i],
            recv_sem=halo_recv.at[i],
            device_id=(tm, to),
            device_id_type=MESH,
        )

    halos = (
        halo(0, g, 2, ROWS + 2, 2, up),
        halo(1, g, ROWS, 0, 2, down),
        halo(2, kept, 1, ROWS + 1, 1, up),
        halo(3, kept, ROWS, 0, 1, down),
    )
    def second_conv(p):
        base = p * PAIR
        out = conv_pair(weight2[...], g, base).astype(BF)
        positive = kept[pl.ds(al(base), PAIR), :] > 0
        pgrad[pl.ds(al(base), PAIR), :] = jnp.where(positive, out, jnp.zeros((), BF))

    def second_grad(p):
        base = p * PAIR + C
        acc2[...] += grad_pair(kept, base, g, base)

    def pass1(s):
        for q in range(1, HALF + 1):
            second_conv(s * HALF + q)
            second_grad(s * HALF + q)

    def get_cot_pre(s):
        fetch(0, s).wait()
        fetch(1, s).wait()
        load_cot_pre(s)

    get_cot_pre(0)
    get_cot_pre(1)
    pass1(0)
    get_cot_pre(STRIPS - 1)
    pl.semaphore_wait(barrier, TM - 1 + 2 * (RING - 1) + 2)
    for h in halos:
        h.start()

    def body1(s, carry):
        get_cot_pre(s + 1)
        pass1(s)
        return carry

    lax.fori_loop(1, STRIPS - 2, body1, 0, unroll=True)
    pass1(STRIPS - 2)
    build_weight(w1_ref, weight1)
    for h in halos:
        h.wait()

    @pl.when(sp == 0)
    def _():
        g[pl.ds(0, 2 * C), :] = jnp.zeros((2 * C, WIDTH), BF)
        kept[pl.ds(0, C), :] = jnp.zeros((C, WIDTH), BF)

    @pl.when(sp == SPACE - 1)
    def _():
        g[pl.ds((ROWS + 2) * C, 2 * C), :] = jnp.zeros((2 * C, WIDTH), BF)
        kept[pl.ds((ROWS + 1) * C, C), :] = jnp.zeros((C, WIDTH), BF)

    for q in range(PAIRS - 7, PAIRS):
        second_conv(q)
        second_grad(q)
    for q in (0, PAIRS):
        second_conv(q)
    second_grad(0)

    def remote(src, dst, send, recv, to):
        return pltpu.make_async_remote_copy(
            src_ref=src, dst_ref=dst, send_sem=send, recv_sem=recv, device_id=to, device_id_type=MESH
        )

    def pack(n, acc):
        tail = []
        for s in range(3):
            top = acc[pl.ds(s * PAIR, C), :][:, : 3 * C]
            both = top + acc[pl.ds(s * PAIR + C, C), :][:, C:]
            flat[pl.ds(n * GRAD_ROWS + s * C, C), :] = both[:, :LANES]
            tail.append(both[:, LANES:])
        tail = jnp.concatenate(tail, axis=0)
        tail = jnp.concatenate([tail[: 3 * C // 2], tail[3 * C // 2 :]], axis=1)
        flat[pl.ds(n * GRAD_ROWS + 3 * C, 3 * C // 2), :] = tail

    scatter = []
    for j in range(1, TM):
        to = lax.rem(tm + j, TM)
        scatter.append(remote(part.at[to], scattered.at[j - 1], rs_send.at[j - 1], rs_recv.at[j - 1], (to, sp)))

    def cross_y(j, slot):
        slot = y if slot is None else lax.rem(y + j, RING)
        return remote(near.at[y], near.at[slot], y_send.at[j], y_recv.at[slot], (tm, y_peer(j)))

    def cross_x(j, slot):
        slot = x if slot is None else lax.rem(x + j, RING)
        return remote(far.at[x], far.at[slot], x_send.at[j], x_recv.at[slot], (tm, x_peer(j)))

    def spread(j, slot):
        to = lax.rem(tm + j, TM)
        slot = tm if slot is None else to
        return remote(total_ref.at[tm], total_ref.at[slot], ag_send.at[j], ag_recv.at[slot], (to, sp))

    def step1():
        for t in range(TM):
            own = jnp.concatenate([flat[pl.ds(t * USED, USED), :], jnp.zeros((CHUNK - USED, LANES), F32)], axis=0)
            part[t] = own.astype(BF)
        for c in scatter:
            c.start()

    def step2():
        for c in scatter:
            c.wait()
        mine = part[tm].astype(F32)
        for j in range(TM - 1):
            mine = mine + scattered[j].astype(F32)
        near[y] = mine.astype(BF)
        for j in range(1, RING):
            cross_y(j, None).start()

    def finish(cross, ref):
        for j in range(1, RING):
            cross(j, None).wait_send()
            cross(j, j).wait_recv()
        whole = ref[0].astype(F32)
        for j in range(1, RING):
            whole = whole + ref[j].astype(F32)
        return whole.astype(BF)

    def step3():
        far[x] = finish(cross_y, near)
        for j in range(1, RING):
            cross_x(j, None).start()

    def step4():
        total_ref[tm] = finish(cross_x, far)
        for j in range(1, TM):
            spread(j, None).start()

    def step5():
        for j in range(1, TM):
            spread(j, None).wait_send()
            spread(j, j).wait_recv()

    def pass2(s):
        for q in range(HALF):
            base = (s * HALF + q) * PAIR
            acc1[...] += grad_pair(inp, base, pgrad, base)

    def get_feat(s):
        fetch(2, s).wait()
        load_feat(s)

    def body2(s, carry):
        get_feat(s + 1)
        pass2(s)
        return carry

    get_feat(0)
    lax.fori_loop(0, STRIPS - 1, body2, 0, unroll=True)
    pass2(STRIPS - 1)
    pack(0, acc1)
    pack(1, acc2)
    step1()

    def store(s):
        r = pl.ds(al(s * STRIP, STRIP), STRIP)
        return pltpu.make_async_copy(cot_in.at[:, r, :], out_hbm.at[:, r, :], out_sem.at[s])

    def body3(s, carry):
        mask = cells[pl.ds(s // 2, 1), :]
        for q in range(HALF):
            base = (s * HALF + q) * PAIR
            kept[pl.ds(al(base), PAIR), :] = (conv_pair(weight1[...], pgrad, base) * mask).astype(BF)
        v = kept[pl.ds(al(s * STRIP * C), STRIP * C), :].reshape(STRIP, C, WIDTH)
        cot_in[:, pl.ds(al(s * STRIP, STRIP), STRIP), :] = jnp.transpose(v, (1, 0, 2))
        store(s).start()
        return carry

    lax.fori_loop(0, 3, body3, 0, unroll=True)
    step2()
    lax.fori_loop(3, 5, body3, 0, unroll=True)
    step3()
    body3(STRIPS - 1, 0)
    step4()
    for s in range(STRIPS):
        store(s).wait()
    step5()


def last_kernel(turned_ref, total_ref, out_hbm, first_ref, second_ref, sem):
    copies = []
    for s in range(PARTS):
        r = pl.ds(s * (C // PARTS), C // PARTS)
        copies.append(pltpu.make_async_copy(turned_ref.at[r], out_hbm.at[r], sem.at[s]))
        copies[-1].start()

    scale = 1.0 / math.sqrt(TM * ROWS * SPACE * WIDTH)
    flat = jnp.concatenate([total_ref[t].astype(F32)[:USED] for t in range(TM)], axis=0)
    for n, ref in enumerate((first_ref, second_ref)):
        rows = flat[n * GRAD_ROWS : (n + 1) * GRAD_ROWS]
        grid = rows[: 3 * C].T * scale
        for q in range(2):
            for s in range(3):
                ref[(2 - q) * 3 + s] = grid[q * C : (q + 1) * C, s * C : (s + 1) * C]
        grid = rows[3 * C :].T * scale
        h = C // 2
        ref[0] = grid[:C, :C]
        ref[1] = jnp.concatenate([grid[:C, C : C + h], grid[C:, :h]], axis=1)
        ref[2] = grid[C:, h : h + C]
    for c in copies:
        c.wait()


def block(features, pre_act, cotangent, first_weight, second_weight, tile_mask, tile_list):
    vmem = pl.BlockSpec(memory_space=pltpu.VMEM)
    hbm = pl.BlockSpec(memory_space=pl.ANY)
    shape = (C, ROWS, WIDTH)
    mask = tile_mask[0].T
    chunk = (CHUNK, LANES)
    dma = pltpu.SemaphoreType.DMA
    turned, total = pl.pallas_call(
        main_kernel,
        out_shape=(
            pltpu.VMEM(shape, BF),
            jax.ShapeDtypeStruct((TM,) + chunk, BF),
        ),
        in_specs=[hbm, hbm, hbm, vmem, vmem, vmem],
        out_specs=(hbm, vmem),
        scratch_shapes=[
            pltpu.VMEM(shape, BF),
            pltpu.VMEM(shape, BF),
            pltpu.VMEM(shape, BF),
            pltpu.VMEM(((ROWS + 4) * C, WIDTH), BF),
            pltpu.VMEM(((ROWS + 2) * C, WIDTH), BF),
            pltpu.VMEM((ROWS * C, WIDTH), BF),
            pltpu.VMEM(((ROWS + 2) * C, WIDTH), BF),
            pltpu.VMEM((3 * PAIR, 2 * PAIR), BF),
            pltpu.VMEM((3 * PAIR, 2 * PAIR), BF),
            pltpu.VMEM((8, WIDTH), F32),
            pltpu.VMEM((3 * PAIR, 2 * PAIR), F32),
            pltpu.VMEM((3 * PAIR, 2 * PAIR), F32),
            pltpu.VMEM((2 * GRAD_ROWS, LANES), F32),
            pltpu.VMEM((TM,) + chunk, BF),
            pltpu.VMEM((TM - 1,) + chunk, BF),
            pltpu.VMEM((RING,) + chunk, BF),
            pltpu.VMEM((RING,) + chunk, BF),
            dma((3, STRIPS)),
            dma((STRIPS,)),
            dma((4,)),
            dma((4,)),
            dma((TM - 1,)),
            dma((TM - 1,)),
            dma((RING,)),
            dma((RING,)),
            dma((RING,)),
            dma((RING,)),
            dma((TM,)),
            dma((TM,)),
        ],
        compiler_params=pltpu.CompilerParams(
            collective_id=0, has_side_effects=True, vmem_limit_bytes=52 * 2**20
        ),
        name="grads",
    )(cotangent[0], pre_act[0], features[0], second_weight, first_weight, mask)
    grad, first, second = pl.pallas_call(
        last_kernel,
        out_shape=(
            jax.ShapeDtypeStruct(shape, BF),
            jax.ShapeDtypeStruct((9, C, C), F32),
            jax.ShapeDtypeStruct((9, C, C), F32),
        ),
        in_specs=[hbm, vmem],
        out_specs=(hbm, vmem, vmem),
        scratch_shapes=[dma((PARTS,))],
        compiler_params=pltpu.CompilerParams(vmem_limit_bytes=8 * 2**20),
        name="input_grad",
    )(turned, total)
    return grad[None], first, second


def solution(mesh):
    return jax.shard_map(
        block,
        mesh=mesh,
        in_specs=(
            P("tm", None, "space", None),
            P("tm", None, "space", None),
            P("tm", None, "space", None),
            P(),
            P(),
            P("tm", None, None),
            P("tm", "space"),
        ),
        out_specs=(P("tm", None, "space", None), P(), P()),
        check_vma=False,
    )
```

time: 69.8 us -> 60.1 us (0.86)
  Pallas kernels: 67.1 us -> 58.2 us
    pallas_call x1, Pallas kernels: 14.4 us -> 3.56 us  [block(): pl.pallas_call(last_kernel, out_shape=(jax.ShapeDtypeStruct(shape, BF), j...]
    pallas_call x1, Pallas kernels: 52.7 us -> 54.7 us  [block(): pl.pallas_call(main_kernel, out_shape=(pltpu.VMEM(shape, BF), jax.ShapeDt...]
where the time goes in v2:
time: 60.1 us; the launch traced here: 59.9 us
  Pallas kernels  58.2 us (97%)
  local copies, waits for them, and re-layouts  0.91 us (2%)
  between operations  0.83 us (1%)
    pallas_call x1, Pallas kernels, block(): pl.pallas_call(main_kernel, out_shape=(pltpu.VMEM(shape, BF), jax.ShapeDt...  54.7 us
    pallas_call x1, Pallas kernels, block(): pl.pallas_call(last_kernel, out_shape=(jax.ShapeDtypeStruct(shape, BF), j...  3.56 us

profile of v2, /device:TPU:1, one launch (start us, length us, event | category | flops | bytes accessed | tf_op | source)
XLA Modules:
  0.0 59.9 jit_solution(15410883754182613747)
XLA Ops:
  0.6 54.7 %grads.1 = (bf16[64,96,512]{2,1,0:T(8,128)(2,1)S(1)}, bf16[8,80,128]{2,1,0:T(8,128)(2,1)}) custom-call(bf16[64,96,512]{2,1,0:T(8,128)(2,1)} %bitcast.7, bf16[64,96,512]{2,1,0:T(8,128)(2,1)} %bitcast.8, bf16[64,96,512]{2,1,0:T(8,128)(2,1)} %bitcast.9, bf16[9,64,64]{2,1,0:T(8,128)(2,1)} %w2_ref.1, bf16[9,64,64]{2,1,0:T(8,128)(2,1)} %w1_ref.1, s32[16,48]{1,0:T(8,128)} %bitcast.10), custom_call_target="tpu_custom_call" | custom-call | tf_op jit(solution)/shard_map/grads/pallas_call | solution.py:379
  55.3 0.0 copy-start
  55.3 0.9 %copy-done = bf16[8,80,128]{2,1,0:T(8,128)(2,1)S(1)} copy-done((bf16[8,80,128]{2,1,0:T(8,128)(2,1)S(1)}, bf16[8,80,128]{2,1,0:T(8,128)(2,1)}, u32[]{:S(2)}) %copy-start) | copy-done | bytes 163864
  56.2 3.6 %input_grad.1 = (bf16[64,96,512]{2,1,0:T(8,128)(2,1)}, f32[9,64,64]{2,1,0:T(8,128)}, f32[9,64,64]{2,1,0:T(8,128)}) custom-call(bf16[64,96,512]{2,1,0:T(8,128)(2,1)S(1)} %get-tuple-element.8.turned_ref, bf16[8,80,128]{2,1,0:T(8,128)(2,1)S(1)} %copy-done), custom_call_target="tpu_custom_call" | custom-call | tf_op jit(solution)/shard_map/input_grad/pallas_call | solution.py:423
Async XLA Ops:
  55.3 0.9 %copy-start = (bf16[8,80,128]{2,1,0:T(8,128)(2,1)S(1)}, bf16[8,80,128]{2,1,0:T(8,128)(2,1)}, u32[]{:S(2)}) copy-start(bf16[8,80,128]{2,1,0:T(8,128)(2,1)} %get-tuple-element.9.total_ref) | copy-start | bytes 491524
